TPU v7x, 32 devices: a whole 2x2x4 slice. The times are simulated.
32 devices in a mesh: blk: 8 (over y, x, core), rep: 4 (over z).
Axes of the slice: x: 2, y: 2, z: 4, core: 2. Of those that a mesh axis runs over, the one named last changes fastest.
Arguments:
- entities: bfloat16 [16384, 256], P('blk'), may hold values from -1.5 to 1.5
- entity_state: float32 [16384], P(('blk', 'rep')), may hold values from 0.05 to 4
- shared_table: bfloat16 [2048, 256], replicated, may hold values from -1.5 to 1.5
- shared_state: float32 [2048], P(('blk', 'rep')), may hold values from 0.05 to 4
- edge_src: int32 [8, 4, 2048], P('blk', None, 'rep'), may hold values from 0 to 2047
- edge_dst: int32 [8, 4, 2048], P('blk', None, 'rep'), may hold values from 0 to 2047
- edge_slot: int32 [8, 4, 2048], P('blk', None, 'rep'), may hold values from 0 to 63
- neg_rows: int32 [8, 4, 16, 512], P('blk', None, 'rep'), may hold values from 0 to 2047
- list_owner: int32 [8, 256, 1], P('blk', 'rep'), may hold values from 0 to 31; in each aligned block of 64 rows (0 to 63, 64 to 127, ..., all dimensions but the last counted through in order) at most 4 rows name the same one
- list_row: int32 [8, 256], P('blk', 'rep'), may hold values from 0 to 63
Outputs:
- new_entities: float32 [16384, 256], P(('blk', 'rep'))
- new_entity_state: float32 [16384], P(('blk', 'rep'))
- new_shared: float32 [2048, 256], P(('blk', 'rep'))
- new_shared_state: float32 [2048], P(('blk', 'rep'))
Inputs may be any that keep to these rules, and one draw needn't show every extreme that they name: Within the 64 list entries of one device (aligned blocks of 64 entries of list_owner), no owner is named more than 4 times, a bound that some block reaches.
All inputs are finite; a program needn't handle non-finite values.
Results may differ from a plain program's by a relative error of at most 0.0022.
Values may be sent and summed in bfloat16 or wider, within the bound.
A program may use at most 64 MiB of HBM per device.

v0:
```python
import jax
import jax.numpy as jnp
from jax import lax
from jax.sharding import PartitionSpec as P

CAP = 4
SH_DEV = 64
LANES = 128


learn_rate = 0.1
negative_weight = 8.0


def passed_along(value, axis, by):
    peers = lax.axis_size(axis)
    return lax.ppermute(value, axis, [(i, (i + by) % peers) for i in range(peers)])


def one_hot(ids, count, dtype=jnp.bfloat16):
    return (ids[..., None] == jnp.arange(count, dtype=jnp.int32)).astype(dtype)


def row_counts(negatives, part_rows):
    high = one_hot(negatives // LANES, part_rows // LANES)
    low = one_hot(negatives % LANES, LANES)
    counts = jnp.einsum("cnh,cnl->chl", high, low, preferred_element_type=jnp.float32)
    return counts.reshape(negatives.shape[0], part_rows)


def scatter_rows(pick, rows):
    return lax.dot_general(
        pick, rows, (((0,), (0,)), ((), ())), preferred_element_type=jnp.float32
    )


def bucket_grads(resident, query, targets, negatives):
    part_rows = resident.shape[0]
    edges = query.shape[0]
    group_count, sample_count = negatives.shape
    counts = row_counts(negatives, part_rows) * (negative_weight / sample_count)
    counts = jnp.repeat(counts, edges // group_count, axis=0)
    scores = lax.dot_general(
        query, resident, (((1,), (1,)), ((), ())), preferred_element_type=jnp.float32
    )
    sigmoid = 0.5 * jnp.tanh(0.5 * scores) + 0.5
    target = one_hot(targets, part_rows, jnp.float32)
    weight = (sigmoid * (counts + target) - target).astype(jnp.bfloat16)
    query_grad = jnp.dot(weight, resident, preferred_element_type=jnp.float32)
    return query_grad.astype(jnp.bfloat16), scatter_rows(weight, query)


def row_adagrad(rows, state, grad):
    new_state = state + jnp.mean(grad * grad, axis=-1)
    return (rows.astype(jnp.float32) - learn_rate * grad / jnp.sqrt(new_state)[:, None], new_state)


def shards(
    entities,
    entity_state,
    shared_table,
    shared_state,
    edge_src,
    edge_dst,
    edge_slot,
    neg_rows,
    list_owner,
    list_row,
):
    rep_count = lax.axis_size("rep")
    rep_place = lax.axis_index("rep")
    device_count = lax.axis_size("blk") * rep_count
    device_place = lax.axis_index("blk") * rep_count + rep_place
    part_rows, model_width = entities.shape
    share_rows = part_rows // rep_count
    bucket_count, edges = edge_src.shape[1:]
    group_count, sample_count = neg_rows.shape[2:]
    owners = list_owner[0, :, 0]
    local_rows = list_row[0]
    slot_count = owners.shape[0]
    ids = []
    for bucket in range(bucket_count):
        own = jnp.concatenate([edge_dst[0, bucket], neg_rows[0, bucket].reshape(-1)])
        ids.append(passed_along(own, "blk", -bucket) if bucket else own)
    shared_rows = shared_table[owners * SH_DEV + local_rows]
    source_picks = [one_hot(edge_src[0, b], part_rows) for b in range(bucket_count)]
    slot_picks = [one_hot(edge_slot[0, b], slot_count) for b in range(bucket_count)]
    queries = []
    for bucket in range(bucket_count):
        source_rows = jnp.dot(source_picks[bucket], entities, preferred_element_type=jnp.float32)
        shared_part = jnp.dot(slot_picks[bucket], shared_rows, preferred_element_type=jnp.float32)
        query = (source_rows + shared_part).astype(jnp.bfloat16)
        queries.append(passed_along(query, "blk", -bucket) if bucket else query)
    grad = jnp.zeros((part_rows, model_width), jnp.float32)
    query_grads = []
    for bucket in range(bucket_count):
        query_grad, target_grad = bucket_grads(
            entities,
            queries[bucket],
            ids[bucket][:edges],
            ids[bucket][edges:].reshape(group_count, sample_count),
        )
        grad = grad + target_grad
        query_grads.append(passed_along(query_grad, "blk", bucket) if bucket else query_grad)
    slot_total = jnp.zeros((slot_count, model_width), jnp.float32)
    for bucket in range(bucket_count):
        grad = grad + scatter_rows(source_picks[bucket], query_grads[bucket])
        slot_total = slot_total + scatter_rows(slot_picks[bucket], query_grads[bucket])
    slot_order = jnp.arange(slot_count, dtype=jnp.int32)
    earlier_same = (owners[:, None] == owners[None, :]) & (
        slot_order[None, :] < slot_order[:, None]
    )
    slot_ranks = jnp.sum(earlier_same.astype(jnp.int32), axis=1)
    send_pick = one_hot(owners * CAP + slot_ranks, device_count * CAP)
    outbound = scatter_rows(send_pick, slot_total.astype(jnp.bfloat16)).astype(jnp.bfloat16)
    labels = scatter_rows(send_pick, local_rows.astype(jnp.bfloat16)[:, None]).astype(jnp.bfloat16)
    outbound = jnp.concatenate(
        [
            outbound.reshape(device_count, CAP * model_width),
            jnp.pad(labels.reshape(device_count, CAP), ((0, 0), (0, LANES - CAP))),
        ],
        axis=1,
    )
    inbound = lax.all_to_all(outbound, ("blk", "rep"), split_axis=0, concat_axis=0, tiled=True)
    own_grad = lax.psum_scatter(
        grad.astype(jnp.bfloat16), "rep", scatter_dimension=0, tiled=True
    ).astype(jnp.float32)
    own_entities = lax.dynamic_slice_in_dim(entities, rep_place * share_rows, share_rows, 0)
    new_entities, new_entity_state = row_adagrad(own_entities, entity_state, own_grad)
    in_rows = inbound[:, : CAP * model_width].reshape(device_count * CAP, model_width)
    in_labels = inbound[:, CAP * model_width : CAP * model_width + CAP].reshape(-1)
    shared_grad = scatter_rows(one_hot(in_labels.astype(jnp.int32), SH_DEV), in_rows)
    own_shared = lax.dynamic_slice_in_dim(shared_table, device_place * SH_DEV, SH_DEV, 0)
    new_shared, new_shared_state = row_adagrad(own_shared, shared_state, shared_grad)
    return (new_entities, new_entity_state, new_shared, new_shared_state)


def solution(mesh):
    return jax.shard_map(
        shards,
        mesh=mesh,
        in_specs=(
            P("blk", None),
            P(("blk", "rep")),
            P(),
            P(("blk", "rep")),
            P("blk", None, "rep"),
            P("blk", None, "rep"),
            P("blk", None, "rep"),
            P("blk", None, "rep", None),
            P("blk", "rep", None),
            P("blk", "rep"),
        ),
        out_specs=(
            P(("blk", "rep"), None),
            P(("blk", "rep")),
            P(("blk", "rep"), None),
            P(("blk", "rep")),
        ),
        check_vma=False,
    )
```

profile of v0, /device:TPU:0, one launch (start us, length us, event | category | flops | bytes accessed | tf_op | source)
XLA Modules:
  0.0 108.5 jit_solution(2924472473680981646)
XLA Ops:
  7.2 0.9 fusion.87
  8.1 0.7 slice_bitcast_fusion.2
  8.8 3.9 %collective-permute-start.3 = (s32[2560]{0:T(1024)S(1)}, s32[2560]{0:T(1024)S(1)}, u32[]{:S(2)}, u32[]{:S(2)}) collective-permute-start(s32[2560]{0:T(1024)S(1)} %pad_add_fusion.1), channel_id=1, source_target_pairs={{0,24},{4,28},{8,0},{12,4},{16,8},{20,12},{24,16},{28,20},{1,25},{... | collective-permute-start | bytes 30728 | tf_op jit(solution)/shard_map/ppermute | solution.py:17
  12.9 1.7 %collective-permute-start.1 = (s32[2560]{0:T(1024)S(1)}, s32[2560]{0:T(1024)S(1)}, u32[]{:S(2)}, u32[]{:S(2)}) collective-permute-start(s32[2560]{0:T(1024)S(1)} %pad_add_fusion), channel_id=1, source_target_pairs={{0,28},{4,0},{8,4},{12,8},{16,12},{20,16},{24,20},{28,24},{1,29},{... | collective-permute-start | bytes 30728 | tf_op jit(solution)/shard_map/ppermute | solution.py:17
  14.6 0.7 fusion.84
  15.3 0.9 fusion.88
  16.1 0.9 fusion.89
  17.0 2.0 %gather_fusion = bf16[64,256]{1,0:T(8,128)(2,1)S(1)} fusion(bf16[2048,256]{1,0:T(8,128)(2,1)} %param.12, s32[1024]{0:T(1024)S(1)} %pad_clamp_fusion), kind=kCustom, calls=%fused_computation | custom fusion | bytes 65792 | tf_op jit(solution)/shard_map/gather | solution.py:85
  19.3 2.9 %fusion.35 = bf16[512,256]{1,0:T(8,128)(2,1)} fusion(f32[512,256]{1,0:T(8,128)S(1)} %fusion.54, bf16[2048,256]{1,0:T(8,128)(2,1)} %param.10, s32[512]{0:T(512)S(1)} %bitcast.155), kind=kOutput, calls=%fused_computation.54 | convolution fusion | flops 538181632 | bytes 1837056 | tf_op jit(solution)/shard_map/dot_general | solution.py:90
  22.5 1.6 %fusion.36 = bf16[512,256]{1,0:T(8,128)(2,1)} fusion(f32[512,256]{1,0:T(8,128)S(1)} %fusion.55, bf16[2048,256]{1,0:T(8,128)(2,1)S(1)} %copy-done, s32[512]{0:T(512)S(1)} %bitcast.149), kind=kOutput, calls=%fused_computation.55 | convolution fusion | flops 538181632 | bytes 1837056 | tf_op jit(solution)/shard_map/dot_general | solution.py:90
  24.1 0.7 collective-permute-start
  24.9 0.7 fusion.43
  25.9 0.9 fusion.37
  26.7 1.7 %fusion.1 = bf16[512,2048]{1,0:T(8,128)(2,1)S(1)} fusion(bf16[512,256]{1,0:T(8,128)(2,1)S(1)} %fusion.37, bf16[2048,256]{1,0:T(8,128)(2,1)S(1)} %copy-done, s32[512]{0:T(512)S(1)} %bitcast.151, f32[4,2048]{1,0:T(4,128)S(1)} %bitcast.137), kind=kOutput, calls=%fused_computation.10 | convolution fusion | flops 546308096 | bytes 3442688 | tf_op jit(solution)/shard_map/dot_general | solution.py:43
  28.4 0.7 convolution_convert_fusion.3
  29.2 0.7 fusion.90
  30.4 2.7 %fusion.14 = f32[2048,256]{1,0:T(8,128)} fusion(bf16[512,256]{1,0:T(8,128)(2,1)S(1)} %convolution_convert_fusion.3, s32[512]{0:T(512)S(1)} %bitcast.160), kind=kOutput, calls=%fused_computation.31 | convolution fusion | flops 537919488 | bytes 2361344 | tf_op jit(solution)/shard_map/dot_general | solution.py:32
  33.1 1.6 %fusion.34 = bf16[512,256]{1,0:T(8,128)(2,1)} fusion(f32[512,256]{1,0:T(8,128)S(1)} %fusion.53, bf16[2048,256]{1,0:T(8,128)(2,1)S(1)} %copy-done, s32[512]{0:T(512)S(1)} %bitcast.157), kind=kOutput, calls=%fused_computation.53 | convolution fusion | flops 538181632 | bytes 1837056 | tf_op jit(solution)/shard_map/dot_general | solution.py:90
  35.0 1.6 %collective-permute-start.4 = (bf16[512,256]{1,0:T(8,128)(2,1)}, bf16[512,256]{1,0:T(8,128)(2,1)S(1)}, u32[]{:S(2)}, u32[]{:S(2)}) collective-permute-start(bf16[512,256]{1,0:T(8,128)(2,1)} %fusion.34), channel_id=1, source_target_pairs={{0,20},{4,24},{8,28},{12,0},{16,4},{20,8},{24,12},{28,16},{1,21},{... | collective-permute-start | bytes 786440 | tf_op jit(solution)/shard_map/ppermute | solution.py:17
  37.3 1.4 %fusion.41 = f32[1,4,16,128]{3,2,1,0:T(8,128)S(1)} fusion(s32[4,512]{1,0:T(4,128)} %get-tuple-element.28, s32[4,512]{1,0:T(4,128)} %get-tuple-element.27), kind=kOutput, calls=%fused_computation.69 | convolution fusion | flops 8691712 | bytes 49152 | tf_op jit(solution)/shard_map/cnh,cnl->chl/dot_general | solution.py:27
  38.7 0.7 fusion.40
  39.5 0.7 fusion.42
  40.2 1.1 collective-permute-done.4
  41.3 1.6 %fusion.7 = bf16[512,2048]{1,0:T(8,128)(2,1)S(1)} fusion(bf16[512,256]{1,0:T(8,128)(2,1)S(1)} %collective-permute-done.4, bf16[2048,256]{1,0:T(8,128)(2,1)S(1)} %copy-done, s32[512]{0:T(512)S(1)} %slice.136, f32[4,2048]{1,0:T(4,128)S(1)} %bitcast.135), kind=kOutput, calls=%fused_computation.16 | convolution fusion | flops 546308096 | bytes 3442688 | tf_op jit(solution)/shard_map/dot_general | solution.py:43
  42.9 0.7 convolution_convert_fusion
  43.6 4.2 %collective-permute-start.8 = (bf16[512,256]{1,0:T(8,128)(2,1)S(1)}, bf16[512,256]{1,0:T(8,128)(2,1)S(1)}, u32[]{:S(2)}, u32[]{:S(2)}) collective-permute-start(bf16[512,256]{1,0:T(8,128)(2,1)S(1)} %convolution_convert_fusion), channel_id=1, source_target_pairs={{0,12},{4,16},{8,20},{12,24},{16,28},{20,0},{24,4},{28,8},{1,13},{... | collective-permute-start | bytes 786440 | tf_op jit(solution)/shard_map/ppermute | solution.py:17
  47.9 2.6 %fusion.3 = bf16[512,2048]{1,0:T(8,128)(2,1)S(1)} fusion(bf16[512,256]{1,0:T(8,128)(2,1)} %collective-permute-done, bf16[2048,256]{1,0:T(8,128)(2,1)S(1)} %copy-done, s32[512]{0:T(512)S(1)} %slice.132, f32[4,2048]{1,0:T(4,128)S(1)} %bitcast.136), kind=kOutput, calls=%fused_computation.12 | convolution fusion | flops 546308096 | bytes 3442688 | tf_op jit(solution)/shard_map/dot_general | solution.py:43
  50.5 0.7 convolution_convert_fusion.2
  51.3 2.6 %fusion.5 = bf16[512,2048]{1,0:T(8,128)(2,1)S(1)} fusion(bf16[512,256]{1,0:T(8,128)(2,1)} %collective-permute-done.2, bf16[2048,256]{1,0:T(8,128)(2,1)S(1)} %copy-done, s32[512]{0:T(512)S(1)} %slice-done, f32[4,2048]{1,0:T(4,128)S(1)} %bitcast.134), kind=kOutput, calls=%fused_computation.14 | convolution fusion | flops 546308096 | bytes 3442688 | tf_op jit(solution)/shard_map/dot_general | solution.py:43
  53.9 0.7 convolution_convert_fusion.1
  54.6 0.7 collective-permute-start.7
  55.3 0.8 fusion.91
  56.0 1.9 %convolution_add_fusion.1 = f32[2048,256]{1,0:T(8,128)S(1)} fusion(f32[2048,256]{1,0:T(8,128)S(1)} %fusion.90, bf16[512,2048]{1,0:T(8,128)(2,1)S(1)} %fusion.3, bf16[512,256]{1,0:T(8,128)(2,1)} %collective-permute-done), kind=kOutput, calls=%fused_computation.36 | convolution fusion | flops 537395200 | bytes 6553600 | tf_op jit(solution)/shard_map/dot_general | solution.py:32
  57.9 1.8 %fusion.18 = f32[2048,256]{1,0:T(8,128)S(1)} fusion(f32[2048,256]{1,0:T(8,128)S(1)} %copy-done.1, f32[2048,256]{1,0:T(8,128)S(1)} %fusion.91, f32[2048,256]{1,0:T(8,128)S(1)} %convolution_add_fusion.1, bf16[512,2048]{1,0:T(8,128)(2,1)S(1)} %fusion.5, bf16[512,256]{1,0:T(8,128)(2,1)} %collective-permute-done.2), kind=kOutput, calls=%fused_computation.37 | convolution fusion | flops 538443776 | bytes 10747904 | tf_op jit(solution)/shard_map/dot_general | solution.py:32
  59.8 1.4 %fusion.8 = f32[2048,256]{1,0:T(8,128)S(1)} fusion(bf16[512,256]{1,0:T(8,128)(2,1)S(1)} %collective-permute-done.8, s32[512]{0:T(512)S(1)} %bitcast.158), kind=kOutput, calls=%fused_computation.19 | convolution fusion | flops 537919488 | bytes 2361344 | tf_op jit(solution)/shard_map/dot_general | solution.py:32
  61.1 3.2 %collective-permute-done.7 = bf16[512,256]{1,0:T(8,128)(2,1)S(1)} collective-permute-done((bf16[512,256]{1,0:T(8,128)(2,1)S(1)}, bf16[512,256]{1,0:T(8,128)(2,1)S(1)}, u32[]{:S(2)}, u32[]{:S(2)}) %collective-permute-start.7) | collective-permute-done | bytes 262176 | tf_op jit(solution)/shard_map/ppermute | solution.py:17
  64.4 1.4 %fusion.10 = f32[2048,256]{1,0:T(8,128)S(1)} fusion(bf16[512,256]{1,0:T(8,128)(2,1)S(1)} %collective-permute-done.7, s32[512]{0:T(512)S(1)} %bitcast.156), kind=kOutput, calls=%fused_computation.23 | convolution fusion | flops 537919488 | bytes 2361344 | tf_op jit(solution)/shard_map/dot_general | solution.py:32
  65.8 0.7 copy-done.2
  66.5 2.6 %fusion.21 = bf16[2048,256]{1,0:T(8,128)(2,1)} fusion(f32[2048,256]{1,0:T(8,128)S(1)} %fusion.8, f32[2048,256]{1,0:T(8,128)S(1)} %fusion.10, f32[2048,256]{1,0:T(8,128)S(1)} %fusion.18, bf16[512,256]{1,0:T(8,128)(2,1)S(1)} %collective-permute-done.6, s32[512]{0:T(512)S(1)} %bitcast.150), kind=kOutput, calls=%fused_computation.40 | convolution fusion | flops 540016640 | bytes 7604224 | tf_op jit(solution)/shard_map/dot_general | solution.py:32
  69.8 1.3 %convolution_add_fusion.3 = f32[64,256]{1,0:T(8,128)S(1)} fusion(f32[64,256]{1,0:T(8,128)S(1)} %fusion.56, bf16[512,256]{1,0:T(8,128)(2,1)} %copy-done.2, s32[512]{0:T(512)S(1)} %bitcast.144), kind=kOutput, calls=%fused_computation.64 | convolution fusion | flops 16826368 | bytes 395264 | tf_op jit(solution)/shard_map/dot_general | solution.py:32
  72.2 0.7 reduce
  72.8 0.8 reshape.213
  73.6 4.9 %all-to-all-start = ((bf16[32,2,576]{2,1,0:T(2,128)(2,1)}), bf16[32,2,576]{2,1,0:T(2,128)(2,1)S(1)}, u32[]{:S(2)}, u32[]{:S(2)}) async-start(bf16[32,2,576]{2,1,0:T(2,128)(2,1)} %reshape.213), calls=%async_computation.1 | async-start | bytes 163840 | tf_op jit(solution)/shard_map/all_to_all | solution.py:124
  78.6 9.0 %all-to-all-done = bf16[32,2,576]{2,1,0:T(2,128)(2,1)S(1)} async-done(((bf16[32,2,576]{2,1,0:T(2,128)(2,1)}), bf16[32,2,576]{2,1,0:T(2,128)(2,1)S(1)}, u32[]{:S(2)}, u32[]{:S(2)}) %all-to-all-start) | async-done | bytes 73760 | tf_op jit(solution)/shard_map/all_to_all | solution.py:124
  88.8 1.5 %divide_subtract_fusion = f32[64,256]{1,0:T(8,128)} fusion(f32[64,256]{1,0:T(8,128)S(1)} %get-tuple-element.32, f32[64]{0:T(128)S(1)} %get-tuple-element.4, bf16[2048,256]{1,0:T(8,128)(2,1)} %param.12, s32[]{:T(128)S(6)} %select_n.67), kind=kLoop, calls=%fused_computation.116 | loop fusion | flops 65536 | bytes 164100 | tf_op jit(solution)/shard_map/sub | solution.py:55
  90.3 7.8 %reduce-scatter.2.cloned.1.call-done = bf16[512,256]{1,0:T(8,128)(2,1)} async-done(((bf16[2048,256]{1,0:T(8,128)(2,1)}), bf16[512,256]{1,0:T(8,128)(2,1)}) %reduce-scatter.2.cloned.1.call-update) | async-done | bytes 262160 | tf_op jit(solution)/shard_map/reduce_scatter | solution.py:125
  98.1 1.1 %fusion.47 = f32[512]{0:T(512)S(1)} fusion(bf16[512,256]{1,0:T(8,128)(2,1)} %reduce-scatter.2.cloned.1.call-done), kind=kLoop, calls=%fused_computation.84 | loop fusion | flops 392704 | bytes 264192 | tf_op jit(solution)/shard_map/reduce_sum | solution.py:54
  99.8 1.9 %fusion.46 = f32[512,256]{1,0:T(8,128)} fusion(bf16[512,256]{1,0:T(8,128)(2,1)} %reduce-scatter.2.cloned.1.call-done, f32[512]{0:T(512)S(1)} %get-tuple-element.6, bf16[2048,256]{1,0:T(8,128)(2,1)S(1)} %copy-done, s32[]{:T(128)S(6)} %select_n.57), kind=kLoop, calls=%fused_computation.83 | loop fusion | flops 655360 | bytes 1050628 | tf_op jit(solution)/shard_map/sub | solution.py:55
  (102 shorter events, 6.3 us)
Async XLA Ops:
  7.2 90.9 %reduce-scatter.2.cloned.1.call-start = ((), (), s32[]{:S(2)}) async-start(), calls=%async_computation.2 | async-start | bytes 1310720 | tf_op jit(solution)/shard_map/reduce_scatter | solution.py:125
  8.8 26.2 %collective-permute-start.3 = (s32[2560]{0:T(1024)S(1)}, s32[2560]{0:T(1024)S(1)}, u32[]{:S(2)}, u32[]{:S(2)}) collective-permute-start(s32[2560]{0:T(1024)S(1)} %pad_add_fusion.1), channel_id=1, source_target_pairs={{0,24},{4,28},{8,0},{12,4},{16,8},{20,12},{24,16},{28,20},{1,25},{... | collective-permute-start | bytes 30728 | tf_op jit(solution)/shard_map/ppermute | solution.py:17
  12.8 24.5 %collective-permute-start.5 = (s32[2560]{0:T(1024)S(1)}, s32[2560]{0:T(1024)S(1)}, u32[]{:S(2)}, u32[]{:S(2)}) collective-permute-start(s32[2560]{0:T(1024)S(1)} %pad_add_fusion.2), channel_id=1, source_target_pairs={{0,20},{4,24},{8,28},{12,0},{16,4},{20,8},{24,12},{28,16},{1,21},{... | collective-permute-start | bytes 30728 | tf_op jit(solution)/shard_map/ppermute | solution.py:17
  12.9 26.6 %collective-permute-start.1 = (s32[2560]{0:T(1024)S(1)}, s32[2560]{0:T(1024)S(1)}, u32[]{:S(2)}, u32[]{:S(2)}) collective-permute-start(s32[2560]{0:T(1024)S(1)} %pad_add_fusion), channel_id=1, source_target_pairs={{0,28},{4,0},{8,4},{12,8},{16,12},{20,16},{24,20},{28,24},{1,29},{... | collective-permute-start | bytes 30728 | tf_op jit(solution)/shard_map/ppermute | solution.py:17
  16.1 6.1 %copy-start.12 = (s32[1,1,512]{2,1,0:T(1,128)}, s32[1,1,512]{2,1,0:T(1,128)S(1)}, u32[]{:S(2)}) copy-start(s32[1,1,512]{2,1,0:T(1,128)S(1)} %get-tuple-element.22) | copy-start | bytes 6148
  16.1 17.0 %copy-start.14 = (s32[1,1,512]{2,1,0:T(1,128)}, s32[1,1,512]{2,1,0:T(1,128)S(1)}, u32[]{:S(2)}) copy-start(s32[1,1,512]{2,1,0:T(1,128)S(1)} %get-tuple-element.21) | copy-start | bytes 6148
  19.3 3.2 %copy-start = (bf16[2048,256]{1,0:T(8,128)(2,1)S(1)}, bf16[2048,256]{1,0:T(8,128)(2,1)}, u32[]{:S(2)}) copy-start(bf16[2048,256]{1,0:T(8,128)(2,1)} %param.10) | copy-start | bytes 3145732
  22.2 29.1 %collective-permute-start.2 = (bf16[512,256]{1,0:T(8,128)(2,1)}, bf16[512,256]{1,0:T(8,128)(2,1)}, u32[]{:S(2)}, u32[]{:S(2)}) collective-permute-start(bf16[512,256]{1,0:T(8,128)(2,1)} %fusion.35), channel_id=1, source_target_pairs={{0,24},{4,28},{8,0},{12,4},{16,8},{20,12},{24,16},{28,20},{1,25},{... | collective-permute-start | bytes 786440 | tf_op jit(solution)/shard_map/ppermute | solution.py:17
  22.5 2.3 %copy-start.9 = (s32[1,4,4,512]{3,2,1,0:T(4,128)S(1)}, s32[1,4,4,512]{3,2,1,0:T(4,128)}, u32[]{:S(2)}) copy-start(s32[1,4,4,512]{3,2,1,0:T(4,128)} %param.17) | copy-start | bytes 98308
  24.1 23.8 %collective-permute-start = (bf16[512,256]{1,0:T(8,128)(2,1)}, bf16[512,256]{1,0:T(8,128)(2,1)}, u32[]{:S(2)}, u32[]{:S(2)}) collective-permute-start(bf16[512,256]{1,0:T(8,128)(2,1)} %fusion.36), channel_id=1, source_target_pairs={{0,28},{4,0},{8,4},{12,8},{16,12},{20,16},{24,20},{28,24},{1,29},{... | collective-permute-start | bytes 786440 | tf_op jit(solution)/shard_map/ppermute | solution.py:17
  29.1 1.3 %copy-start.3 = (bf16[512,256]{1,0:T(8,128)(2,1)}, bf16[512,256]{1,0:T(8,128)(2,1)S(1)}, u32[]{:S(2)}) copy-start(bf16[512,256]{1,0:T(8,128)(2,1)S(1)} %convolution_convert_fusion.3) | copy-start | bytes 786436
  29.1 0.8 copy-start.19
  30.1 4.6 %copy-start.17 = (s32[64]{0:T(128)}, s32[64]{0:T(128)S(1)}, u32[]{:S(2)}) copy-start(s32[64]{0:T(128)S(1)} %multiply_add_fusion.2) | copy-start | bytes 772
  33.1 1.6 %copy-start.20 = (s32[1,64]{1,0:T(1,128)S(1)}, s32[1,64]{1,0:T(1,128)}, u32[]{:S(2)}) copy-start(s32[1,64]{1,0:T(1,128)} %param.19) | copy-start | bytes 772
  35.0 7.9 %copy-start.10 = (s32[2560]{0:T(1024)}, s32[2560]{0:T(1024)S(1)}, u32[]{:S(2)}) copy-start(s32[2560]{0:T(1024)S(1)} %collective-permute-done.3) | copy-start | bytes 30724
  35.0 6.2 %collective-permute-start.4 = (bf16[512,256]{1,0:T(8,128)(2,1)}, bf16[512,256]{1,0:T(8,128)(2,1)S(1)}, u32[]{:S(2)}, u32[]{:S(2)}) collective-permute-start(bf16[512,256]{1,0:T(8,128)(2,1)} %fusion.34), channel_id=1, source_target_pairs={{0,20},{4,24},{8,28},{12,0},{16,4},{20,8},{24,12},{28,16},{1,21},{... | collective-permute-start | bytes 786440 | tf_op jit(solution)/shard_map/ppermute | solution.py:17
  43.6 16.1 %collective-permute-start.8 = (bf16[512,256]{1,0:T(8,128)(2,1)S(1)}, bf16[512,256]{1,0:T(8,128)(2,1)S(1)}, u32[]{:S(2)}, u32[]{:S(2)}) collective-permute-start(bf16[512,256]{1,0:T(8,128)(2,1)S(1)} %convolution_convert_fusion), channel_id=1, source_target_pairs={{0,12},{4,16},{8,20},{12,24},{16,28},{20,0},{24,4},{28,8},{1,13},{... | collective-permute-start | bytes 786440 | tf_op jit(solution)/shard_map/ppermute | solution.py:17
  50.5 0.8 slice-start
  51.2 14.6 %collective-permute-start.6 = (bf16[512,256]{1,0:T(8,128)(2,1)S(1)}, bf16[512,256]{1,0:T(8,128)(2,1)S(1)}, u32[]{:S(2)}, u32[]{:S(2)}) collective-permute-start(bf16[512,256]{1,0:T(8,128)(2,1)S(1)} %convolution_convert_fusion.2), channel_id=1, source_target_pairs={{0,4},{4,8},{8,12},{12,16},{16,20},{20,24},{24,28},{28,0},{1,5},{5... | collective-permute-start | bytes 786440 | tf_op jit(solution)/shard_map/ppermute | solution.py:17
  54.6 9.8 %collective-permute-start.7 = (bf16[512,256]{1,0:T(8,128)(2,1)S(1)}, bf16[512,256]{1,0:T(8,128)(2,1)S(1)}, u32[]{:S(2)}, u32[]{:S(2)}) collective-permute-start(bf16[512,256]{1,0:T(8,128)(2,1)S(1)} %convolution_convert_fusion.1), channel_id=1, source_target_pairs={{0,8},{4,12},{8,16},{12,20},{16,24},{20,28},{24,0},{28,4},{1,9},{5... | collective-permute-start | bytes 786440 | tf_op jit(solution)/shard_map/ppermute | solution.py:17
  56.0 1.9 %copy-start.1 = (f32[2048,256]{1,0:T(8,128)S(1)}, f32[2048,256]{1,0:T(8,128)}, u32[]{:S(2)}) copy-start(f32[2048,256]{1,0:T(8,128)} %fusion.14) | copy-start | bytes 6291460
  57.9 1.8 %copy-start.15 = (s32[1,1,512]{2,1,0:T(1,128)S(1)}, s32[1,1,512]{2,1,0:T(1,128)}, u32[]{:S(2)}) copy-start(s32[1,1,512]{2,1,0:T(1,128)} %copy-done.14) | copy-start | bytes 6148
  59.7 4.7 %copy-start.13 = (s32[1,1,512]{2,1,0:T(1,128)S(1)}, s32[1,1,512]{2,1,0:T(1,128)}, u32[]{:S(2)}) copy-start(s32[1,1,512]{2,1,0:T(1,128)} %copy-done.12) | copy-start | bytes 6148
  59.7 6.0 %copy-start.5 = (bf16[512,256]{1,0:T(8,128)(2,1)}, bf16[512,256]{1,0:T(8,128)(2,1)S(1)}, u32[]{:S(2)}) copy-start(bf16[512,256]{1,0:T(8,128)(2,1)S(1)} %collective-permute-done.8) | copy-start | bytes 786436
  64.4 1.4 %copy-start.7 = (bf16[512,256]{1,0:T(8,128)(2,1)}, bf16[512,256]{1,0:T(8,128)(2,1)S(1)}, u32[]{:S(2)}) copy-start(bf16[512,256]{1,0:T(8,128)(2,1)S(1)} %collective-permute-done.7) | copy-start | bytes 786436
  65.8 3.4 %copy-start.4 = (bf16[512,256]{1,0:T(8,128)(2,1)S(1)}, bf16[512,256]{1,0:T(8,128)(2,1)}, u32[]{:S(2)}) copy-start(bf16[512,256]{1,0:T(8,128)(2,1)} %copy-done.3) | copy-start | bytes 786436
  65.8 0.7 copy-start.2
  66.5 3.0 %copy-start.6 = (bf16[512,256]{1,0:T(8,128)(2,1)S(1)}, bf16[512,256]{1,0:T(8,128)(2,1)}, u32[]{:S(2)}) copy-start(bf16[512,256]{1,0:T(8,128)(2,1)} %copy-done.5) | copy-start | bytes 786436
  69.1 2.0 %copy-start.8 = (bf16[512,256]{1,0:T(8,128)(2,1)S(1)}, bf16[512,256]{1,0:T(8,128)(2,1)}, u32[]{:S(2)}) copy-start(bf16[512,256]{1,0:T(8,128)(2,1)} %copy-done.7) | copy-start | bytes 786436
  69.1 2.0 %copy-start.18 = (s32[64]{0:T(128)S(1)}, s32[64]{0:T(128)}, u32[]{:S(2)}) copy-start(s32[64]{0:T(128)} %copy-done.17) | copy-start | bytes 772
  69.1 19.2 %copy-start.16 = (f32[64]{0:T(128)S(1)}, f32[64]{0:T(128)}, u32[]{:S(2)}) copy-start(f32[64]{0:T(128)} %param.13) | copy-start | bytes 772
  69.1 30.1 %copy-start.11 = (f32[512]{0:T(512)S(1)}, f32[512]{0:T(512)}, u32[]{:S(2)}) copy-start(f32[512]{0:T(512)} %param.11) | copy-start | bytes 6148
  73.6 14.0 %all-to-all-start = ((bf16[32,2,576]{2,1,0:T(2,128)(2,1)}), bf16[32,2,576]{2,1,0:T(2,128)(2,1)S(1)}, u32[]{:S(2)}, u32[]{:S(2)}) async-start(bf16[32,2,576]{2,1,0:T(2,128)(2,1)} %reshape.213), calls=%async_computation.1 | async-start | bytes 163840 | tf_op jit(solution)/shard_map/all_to_all | solution.py:124
Sparse Core Ops, SparseCore 0:
  69.2 28.7 reduce-scatter.1
where the time goes:
time: 109 us
  matrix products  38.8 us (36%)
  waiting for transfers between devices  21.1 us (19%)
  starting transfers between devices  18 us (17%)
  between operations  14.7 us (13%)
  local copies, waits for them, and re-layouts  8.06 us (7%)
  other arithmetic  7.82 us (7%)
    dot_general x14, matrix products, scatter_rows(): lax.dot_general(pick, rows, (((0,), (0,)), ((), ())), preferred_element_t...  16.1 us
    ppermute x9, starting transfers between devices, passed_along(): lax.ppermute(value, axis, [(i, (i + by) % peers) for i in range(peers)])  13 us
    all_to_all x1, waiting for transfers between devices, shards(): lax.all_to_all(outbound, ('blk', 'rep'), split_axis=0, concat_axis=0, til...  9.02 us
    dot_general x4, matrix products, bucket_grads(): lax.dot_general(query, resident, (((1,), (1,)), ((), ())), preferred_elem...  8.49 us
    reduce_scatter x1, waiting for transfers between devices, shards(): lax.psum_scatter(grad.astype(jnp.bfloat16), 'rep', scatter_dimension=0, t...  7.77 us
    dot_general x4, matrix products, shards(): jnp.dot(source_picks[bucket], entities, preferred_element_type=jnp.float32)  6.89 us
    all_to_all x1, starting transfers between devices, shards(): lax.all_to_all(outbound, ('blk', 'rep'), split_axis=0, concat_axis=0, til...  4.92 us
    ppermute x9, waiting for transfers between devices, passed_along(): lax.ppermute(value, axis, [(i, (i + by) % peers) for i in range(peers)])  4.33 us
  transfers between devices with their start and end apart: 11, of which 4 were waited for; matrix products, arithmetic and copies ran while one was open for 42% of the time, Pallas kernels for 0%

commit v1 on v0

v1 whole, which is shorter than its diff:
```python
import functools

import jax
import jax.numpy as jnp
from jax import lax
from jax.experimental import pallas as pl
from jax.experimental.pallas import tpu as pltpu
from jax.sharding import PartitionSpec as P

CAP = 4
SH_DEV = 64
LANES = 128
CHUNK = 512
SLAB = 8


learn_rate = 0.1
negative_weight = 8.0
MESH = pl.DeviceIdType.MESH
f32 = jnp.float32
bf16 = jnp.bfloat16


def dot(a, b):
    return jnp.dot(a, b, preferred_element_type=f32)


def dot_split(a, b):
    high = b.astype(bf16)
    low = (b - high.astype(f32)).astype(bf16)
    return dot(a, high) + dot(a, low)


def columns(row):
    return jnp.transpose(jnp.broadcast_to(row.astype(f32), (LANES, row.shape[1])))


def tiled(cols, width):
    return jnp.concatenate([cols] * (width // LANES), axis=1)


def lane_hot(cols, start, width):
    ids = lax.broadcasted_iota(jnp.int32, (cols.shape[0], width), 1) + start
    return tiled(cols, width) == ids.astype(f32)


def kernel(
    groups,
    ent_ref,
    table_ref,
    ids_ref,
    list_ref,
    ent_state_ref,
    sh_state_ref,
    new_ent_ref,
    new_ent_state_ref,
    new_sh_ref,
    new_sh_state_ref,
    vt_ref,
    pick_ref,
    slot_ref,
    q_out,
    q_in,
    ids_in,
    qg_out,
    qg_in,
    dcol_ref,
    cnt_ref,
    qg_ref,
    gt_ref,
    rs_out,
    rs_in,
    sh_out,
    sh_in,
    q_send,
    q_recv,
    i_send,
    i_recv,
    g_send,
    g_recv,
    r_send,
    r_recv,
    s_send,
    s_recv,
):
    blk, rep = lax.axis_index("blk"), lax.axis_index("rep")
    blks, reps = lax.axis_size("blk"), lax.axis_size("rep")
    devices = blks * reps
    me = blk * reps + rep
    rows, width = ent_ref.shape
    buckets, edges = ids_ref.shape[0], ids_ref.shape[2]
    group_edges = edges // groups
    chunks = rows // CHUNK
    highs = rows // LANES
    share = rows // reps
    list_pad = list_ref.shape[1]

    def place(peer):
        return (peer // reps, lax.rem(peer, reps))

    barrier = pltpu.get_barrier_semaphore()

    def greet(off, _):
        pl.semaphore_signal(
            barrier,
            inc=1,
            device_id=place(lax.rem(me + off, devices)),
            device_id_type=MESH,
        )
        return 0

    lax.fori_loop(1, devices, greet, 0)

    vt_ref[...] = jnp.transpose(ent_ref[...].astype(f32)).astype(bf16)
    id_cols = columns(list_ref[0:1, :])
    shared_rows = jnp.zeros((list_pad, width), f32)
    step = min(2048, table_ref.shape[0])
    for start in range(0, table_ref.shape[0], step):
        hot = jnp.where(lane_hot(id_cols, start, step), 1.0, 0.0).astype(bf16)
        shared_rows = shared_rows + dot(hot, table_ref[start : start + step, :])
    shared_rows = shared_rows.astype(bf16)

    def to_back(bucket):
        return (lax.rem(blk - bucket + blks, blks), rep)

    def to_front(bucket):
        return (lax.rem(blk + bucket, blks), rep)

    def id_copy(bucket):
        return pltpu.make_async_remote_copy(
            src_ref=ids_ref.at[bucket],
            dst_ref=ids_in.at[bucket],
            send_sem=i_send.at[bucket],
            recv_sem=i_recv.at[bucket],
            device_id=to_back(bucket),
            device_id_type=MESH,
        )

    def query_copy(bucket):
        return pltpu.make_async_remote_copy(
            src_ref=q_out.at[bucket],
            dst_ref=q_in.at[bucket],
            send_sem=q_send.at[bucket],
            recv_sem=q_recv.at[bucket],
            device_id=to_back(bucket),
            device_id_type=MESH,
        )

    def grad_copy(bucket):
        return pltpu.make_async_remote_copy(
            src_ref=qg_out.at[bucket],
            dst_ref=qg_in.at[bucket],
            send_sem=g_send.at[bucket],
            recv_sem=g_recv.at[bucket],
            device_id=to_front(bucket),
            device_id_type=MESH,
        )

    def make_query(bucket):
        slot = jnp.where(lane_hot(columns(ids_ref[bucket, 6:7, :]), 0, list_pad), 1.0, 0.0)
        slot_ref[bucket] = slot.astype(bf16)
        dcol_ref[...] = columns(ids_ref[bucket, 5:6, :])
        qg_ref[...] = dot(slot_ref[bucket], shared_rows)

        def body(c, _):
            at = pl.multiple_of(c * CHUNK, CHUNK)
            pick = jnp.where(lane_hot(dcol_ref[...], at, CHUNK), 1.0, 0.0).astype(bf16)
            pick_ref[bucket, :, pl.ds(at, CHUNK)] = pick
            qg_ref[...] += dot(pick, ent_ref[pl.ds(at, CHUNK), :])
            return 0

        lax.fori_loop(0, chunks, body, 0)
        q_out[bucket] = qg_ref[...].astype(bf16)

    def score(query_ref, id_ref, out_ref, first):
        query = query_ref[...]
        query_t = jnp.transpose(query.astype(f32)).astype(bf16)
        dcol_ref[...] = columns(id_ref[0:1, :])
        for g in range(groups):
            ids = id_ref[1 + g : 2 + g, :]
            high = lax.broadcasted_iota(jnp.int32, (highs, ids.shape[1]), 0) == ids // LANES
            low = lax.broadcasted_iota(jnp.int32, (LANES, ids.shape[1]), 0) == lax.rem(ids, LANES)
            counts = lax.dot_general(
                jnp.where(high, 1.0, 0.0).astype(bf16),
                jnp.where(low, 1.0, 0.0).astype(bf16),
                (((1,), (1,)), ((), ())),
                preferred_element_type=f32,
            )
            cnt_ref[g * highs : (g + 1) * highs, :] = counts * (negative_weight / ids.shape[1])
        qg_ref[...] = jnp.zeros_like(qg_ref)

        def body(c, _):
            at = pl.multiple_of(c * CHUNK, CHUNK)
            scores = dot(query, vt_ref[:, pl.ds(at, CHUNK)])
            sigmoid = 0.5 * jnp.tanh(0.5 * scores) + 0.5
            per = CHUNK // LANES
            counts = jnp.concatenate(
                [
                    jnp.concatenate(
                        [
                            jnp.broadcast_to(
                                cnt_ref[pl.ds(g * highs + c * per + h, 1), :],
                                (group_edges, LANES),
                            )
                            for h in range(per)
                        ],
                        axis=1,
                    )
                    for g in range(groups)
                ],
                axis=0,
            )
            target = lane_hot(dcol_ref[...], at, CHUNK)
            sampled = sigmoid * counts
            weight = jnp.where(target, sampled + sigmoid - 1.0, sampled).astype(bf16)
            qg_ref[...] += dot(weight, ent_ref[pl.ds(at, CHUNK), :])
            grown = dot(query_t, weight)
            if first:
                gt_ref[:, pl.ds(at, CHUNK)] = grown
            else:
                gt_ref[:, pl.ds(at, CHUNK)] += grown
            return 0

        lax.fori_loop(0, chunks, body, 0)
        out_ref[...] = jnp.transpose(qg_ref[...]).astype(bf16)

    make_query(1)
    pl.semaphore_wait(barrier, devices - 1)
    for bucket in range(1, buckets):
        id_copy(bucket).start()
    for bucket in range(1, buckets):
        if bucket > 1:
            make_query(bucket)
        query_copy(bucket).start()
    make_query(0)
    score(q_out.at[0], ids_ref.at[0], qg_out.at[0], True)
    for bucket in range(1, buckets):
        id_copy(bucket).wait_recv()
        query_copy(bucket).wait_recv()
        score(q_in.at[bucket], ids_in.at[bucket], qg_out.at[bucket], False)
        grad_copy(bucket).start()

    slot_total = jnp.zeros((width, list_pad), f32)
    for bucket in range(buckets):
        if bucket:
            grad_copy(bucket).wait_recv()
            back = qg_in[bucket]
        else:
            back = qg_out[0]
        slot_total = slot_total + dot(back, slot_ref[bucket])

        def body(c, _, back=back, bucket=bucket):
            at = pl.ds(pl.multiple_of(c * CHUNK, CHUNK), CHUNK)
            gt_ref[:, at] += dot(back, pick_ref[bucket, :, at])
            return 0

        lax.fori_loop(0, chunks, body, 0)

    def share_copy(peer):
        return pltpu.make_async_remote_copy(
            src_ref=rs_out.at[peer],
            dst_ref=rs_in.at[rep],
            send_sem=r_send.at[peer],
            recv_sem=r_recv.at[rep],
            device_id=(blk, peer),
            device_id_type=MESH,
        )

    for off in range(1, reps):
        peer = lax.rem(rep + off, reps)
        at = pl.ds(pl.multiple_of(peer * share, share), share)
        rs_out[peer] = gt_ref[:, at].astype(bf16)
        share_copy(peer).start()

    keys = list_ref[1:2, :]
    hot = lax.broadcasted_iota(jnp.int32, (devices * SLAB, list_pad), 0) == keys
    sh_out[:, :width] = dot_split(
        jnp.where(hot, 1.0, 0.0).astype(bf16), jnp.transpose(slot_total)
    )
    marks = jnp.where(hot, list_ref[2:3, :].astype(f32), 0.0).astype(bf16)
    sh_out[:, width:] = dot(marks, jnp.ones((list_pad, LANES), bf16))

    def slab(ref, peer):
        return ref.at[pl.ds(pl.multiple_of(peer * SLAB, SLAB), SLAB), :]

    def slab_copy(peer):
        return pltpu.make_async_remote_copy(
            src_ref=slab(sh_out, peer),
            dst_ref=slab(sh_in, me),
            send_sem=s_send.at[peer],
            recv_sem=s_recv.at[me],
            device_id=place(peer),
            device_id_type=MESH,
        )

    def slab_start(off, _):
        slab_copy(lax.rem(me + off, devices)).start()
        return 0

    lax.fori_loop(1, devices, slab_start, 0)
    own = pl.ds(pl.multiple_of(me * SLAB, SLAB), SLAB)
    sh_in[own, :] = sh_out[own, :]

    def slab_wait(off, _):
        peer = lax.rem(me + off, devices)
        pltpu.make_async_remote_copy(
            src_ref=slab(sh_out, peer),
            dst_ref=slab(sh_in, peer),
            send_sem=s_send.at[peer],
            recv_sem=s_recv.at[peer],
            device_id=place(peer),
            device_id_type=MESH,
        ).wait()
        return 0

    lax.fori_loop(1, devices, slab_wait, 0)
    labels = jnp.transpose(sh_in[:, width:])[:SH_DEV, :]
    hot = labels == lax.broadcasted_iota(jnp.int32, labels.shape, 0).astype(f32)
    shared_grad = dot_split(jnp.where(hot, 1.0, 0.0).astype(bf16), sh_in[:, :width])
    new_state = sh_state_ref[...] + jnp.mean(shared_grad * shared_grad, axis=1, keepdims=True)
    new_sh_state_ref[...] = new_state
    own_shared = table_ref[pl.ds(pl.multiple_of(me * SH_DEV, SH_DEV), SH_DEV), :].astype(f32)
    new_sh_ref[...] = own_shared - learn_rate * shared_grad / jnp.sqrt(new_state)

    own = pl.ds(pl.multiple_of(rep * share, share), share)
    grad = gt_ref[:, own]
    for off in range(1, reps):
        peer = lax.rem(rep + reps - off, reps)
        pltpu.make_async_remote_copy(
            src_ref=rs_out.at[peer],
            dst_ref=rs_in.at[peer],
            send_sem=r_send.at[peer],
            recv_sem=r_recv.at[peer],
            device_id=(blk, peer),
            device_id_type=MESH,
        ).wait()
        grad = grad + rs_in[peer].astype(f32)
    new_state = ent_state_ref[...] + jnp.mean(grad * grad, axis=0, keepdims=True)
    new_ent_state_ref[...] = new_state
    update = jnp.transpose(learn_rate * grad / jnp.sqrt(new_state))
    new_ent_ref[...] = ent_ref[own, :].astype(f32) - update
    for bucket in range(1, buckets):
        id_copy(bucket).wait_send()
        query_copy(bucket).wait_send()
        grad_copy(bucket).wait_send()


def shards(
    entities,
    entity_state,
    shared_table,
    shared_state,
    edge_src,
    edge_dst,
    edge_slot,
    neg_rows,
    list_owner,
    list_row,
):
    reps = lax.axis_size("rep")
    devices = lax.axis_size("blk") * reps
    rows, width = entities.shape
    share = rows // reps
    buckets, edges = edge_src.shape[1:]
    groups = neg_rows.shape[2]
    owners = list_owner[0, :, 0]
    count = owners.shape[0]
    list_pad = -(-count // LANES) * LANES
    order = jnp.arange(count, dtype=jnp.int32)
    earlier = (owners[:, None] == owners[None, :]) & (order[:, None] < order[None, :])
    ranks = jnp.sum(earlier.astype(jnp.int32), axis=0)
    lists = jnp.stack([owners * SH_DEV + list_row[0], owners * SLAB + ranks, list_row[0]])
    lists = jnp.pad(lists, ((0, 5), (0, list_pad - count)), constant_values=-1)
    ids = jnp.concatenate(
        [
            edge_dst[0][:, None],
            neg_rows[0],
            edge_src[0][:, None],
            edge_slot[0][:, None],
            jnp.zeros((buckets, 1, edges), jnp.int32),
        ],
        axis=1,
    )
    sems = pltpu.SemaphoreType.DMA
    vmem = pl.BlockSpec(memory_space=pltpu.VMEM)
    new_entities, new_entity_state, new_shared, new_shared_state = pl.pallas_call(
        functools.partial(kernel, groups),
        out_shape=(
            jax.ShapeDtypeStruct((share, width), f32),
            jax.ShapeDtypeStruct((1, share), f32),
            jax.ShapeDtypeStruct((SH_DEV, width), f32),
            jax.ShapeDtypeStruct((SH_DEV, 1), f32),
        ),
        in_specs=[vmem] * 6,
        out_specs=[vmem] * 4,
        scratch_shapes=[
            pltpu.VMEM((width, rows), bf16),
            pltpu.VMEM((buckets, edges, rows), bf16),
            pltpu.VMEM((buckets, edges, list_pad), bf16),
            pltpu.VMEM((buckets, edges, width), bf16),
            pltpu.VMEM((buckets, edges, width), bf16),
            pltpu.VMEM((buckets, 8, edges), jnp.int32),
            pltpu.VMEM((buckets, width, edges), bf16),
            pltpu.VMEM((buckets, width, edges), bf16),
            pltpu.VMEM((edges, LANES), f32),
            pltpu.VMEM((groups * (rows // LANES), LANES), f32),
            pltpu.VMEM((edges, width), f32),
            pltpu.VMEM((width, rows), f32),
            pltpu.VMEM((reps, width, share), bf16),
            pltpu.VMEM((reps, width, share), bf16),
            pltpu.VMEM((devices * SLAB, width + LANES), f32),
            pltpu.VMEM((devices * SLAB, width + LANES), f32),
            sems((buckets,)),
            sems((buckets,)),
            sems((buckets,)),
            sems((buckets,)),
            sems((buckets,)),
            sems((buckets,)),
            sems((reps,)),
            sems((reps,)),
            sems((devices,)),
            sems((devices,)),
        ],
        compiler_params=pltpu.CompilerParams(
            collective_id=0, has_side_effects=True, vmem_limit_bytes=56 * 2**20
        ),
    )(
        entities,
        shared_table,
        ids,
        lists,
        entity_state.reshape(1, share),
        shared_state.reshape(SH_DEV, 1),
    )
    return (
        new_entities,
        new_entity_state.reshape(share),
        new_shared,
        new_shared_state.reshape(SH_DEV),
    )


def solution(mesh):
    return jax.shard_map(
        shards,
        mesh=mesh,
        in_specs=(
            P("blk", None),
            P(("blk", "rep")),
            P(),
            P(("blk", "rep")),
            P("blk", None, "rep"),
            P("blk", None, "rep"),
            P("blk", None, "rep"),
            P("blk", None, "rep", None),
            P("blk", "rep", None),
            P("blk", "rep"),
        ),
        out_specs=(
            P(("blk", "rep"), None),
            P(("blk", "rep")),
            P(("blk", "rep"), None),
            P(("blk", "rep")),
        ),
        check_vma=False,
    )
```

time: 109 us -> 80.1 us (0.73)
  Pallas kernels: 0 us -> 71.1 us
  matrix products: 38.8 us -> 0 us
  waiting for transfers between devices: 21.1 us -> 0 us
  starting transfers between devices: 18 us -> 0 us
  between operations: 14.7 us -> 0.7 us
  other arithmetic: 7.82 us -> 1.49 us
  local copies, waits for them, and re-layouts: 8.06 us -> 6.47 us
    pallas_call x0 -> x1, Pallas kernels: none -> 71.1 us  [shards(): pl.pallas_call(functools.partial(kernel, groups), out_shape=(jax.ShapeDty...]
    dot_general x34 -> x0, matrix products: 38.8 us -> none  [the longest x14 16.1 us: scatter_rows(): lax.dot_general(pick, rows, (((0,), (0,)), ((), ())), preferred_element_t...]
    ppermute x9 -> x0, starting transfers between devices: 13 us -> none  [passed_along(): lax.ppermute(value, axis, [(i, (i + by) % peers) for i in range(peers)])]
    all_to_all x1 -> x0, waiting for transfers between devices: 9.02 us -> none  [shards(): lax.all_to_all(outbound, ('blk', 'rep'), split_axis=0, concat_axis=0, til...]
    reduce_scatter x1 -> x0, waiting for transfers between devices: 7.77 us -> none  [shards(): lax.psum_scatter(grad.astype(jnp.bfloat16), 'rep', scatter_dimension=0, t...]
    all_to_all x1 -> x0, starting transfers between devices: 4.92 us -> none  [shards(): lax.all_to_all(outbound, ('blk', 'rep'), split_axis=0, concat_axis=0, til...]
    ppermute x9 -> x0, waiting for transfers between devices: 4.33 us -> none  [passed_along(): lax.ppermute(value, axis, [(i, (i + by) % peers) for i in range(peers)])]
    sub x2 -> x0, other arithmetic: 3.38 us -> none  [row_adagrad(): rows.astype(jnp.float32) - learn_rate * grad / jnp.sqrt(new_state)[:, None]]
  transfers between devices with their start and end apart: 11 -> 0, of which waited for: 4 -> 0; matrix products, arithmetic and copies ran while one was open for 42% -> 0% of each run, Pallas kernels for 0% -> 0%
where the time goes in v1:
time: 80.1 us; the launch traced here: 79.7 us
  Pallas kernels  71.1 us (89%)
  local copies, waits for them, and re-layouts  6.47 us (8%)
  other arithmetic  1.49 us (2%)
    pallas_call x1, Pallas kernels, shards(): pl.pallas_call(functools.partial(kernel, groups), out_shape=(jax.ShapeDty...  71.1 us
    unnamed x21, local copies, waits for them, and re-layouts  4.45 us

profile of v1, /device:TPU:0, one launch (start us, length us, event | category | flops | bytes accessed | tf_op | source)
XLA Modules:
  0.0 79.7 jit_solution(6544246480860902403)
XLA Ops:
  0.6 0.0 copy-start.8
  0.6 0.6 copy-done.8
  1.3 0.0 copy-start.5
  1.3 0.1 convert_reduce_fusion
  1.4 0.6 copy-done.5
  1.9 0.0 copy-start.2
  1.9 0.0 copy-start.3
  2.0 0.0 copy-start.4
  2.0 0.0 copy-start.1
  2.0 0.6 pad.4.list_ref
  2.6 0.1 copy-done.2
  2.6 0.0 copy-done.3
  2.7 0.0 copy-done.4
  2.7 0.0 copy-done.1
  2.8 0.0 copy-start.7
  2.8 0.7 concatenate.3.ids_ref
  3.4 0.0 copy-done.7
  3.5 0.7 copy.16.sh_state_ref
  4.2 71.1 %shard_map.129 = (f32[512,256]{1,0:T(8,128)}, f32[1,512]{1,0:T(1,128)}, f32[64,256]{1,0:T(8,128)}, f32[64,1]{1,0:T(8,128)}) custom-call(bf16[2048,256]{1,0:T(8,128)(2,1)} %ent_ref.1, bf16[2048,256]{1,0:T(8,128)(2,1)} %table_ref.1, s32[4,8,512]{2,1,0:T(8,128)} %concatenate.3.ids_ref, s32[8,128]{1,0:T(8,128)} %pad.4.list_ref, f32[1,512]{1,0:T(1,128)} %bitcast.12, ...), custom_call_target="tpu_custom_call" | custom-call | tf_op jit(solution)/shard_map/pallas_call | solution.py:386
  75.2 1.4 %reduce = f32[64]{0:T(128)} reduce(f32[64,1]{1,0:T(8,128)} %get-tuple-element.11, f32[]{:T(128)} %constant.17), dimensions={1}, to_apply=%get-tuple-element.11.reduce_sub_computation | reduce | bytes 516 | tf_op jit(solution)/shard_map/pallas_call | solution.py:386
  76.6 0.0 copy-start.6
  76.6 0.0 copy-start
  76.6 1.9 %copy.20 = f32[512,256]{1,0:T(8,128)} copy(f32[512,256]{1,0:T(8,128)} %get-tuple-element.18) | data formatting | bytes 1048576
  78.5 0.0 copy-done.6
  78.5 0.6 copy.21
  79.1 0.0 copy-done
  79.1 0.6 copy.22
  (6 shorter events, 0.0 us)
Async XLA Ops:
  0.6 0.7 copy-start.8
  1.3 0.7 copy-start.5
  1.9 0.7 copy-start.2
  1.9 0.7 copy-start.3
  2.0 0.7 copy-start.4
  2.0 0.8 copy-start.1
  2.8 0.7 copy-start.7
  76.6 1.9 %copy-start.6 = (f32[1,512]{1,0:T(1,128)S(1)}, f32[1,512]{1,0:T(1,128)}, u32[]{:S(2)}) copy-start(f32[1,512]{1,0:T(1,128)} %get-tuple-element.9) | copy-start | bytes 6148
  76.6 2.5 %copy-start = (f32[64,256]{1,0:T(8,128)S(1)}, f32[64,256]{1,0:T(8,128)}, u32[]{:S(2)}) copy-start(f32[64,256]{1,0:T(8,128)} %get-tuple-element.20) | copy-start | bytes 196612

commit v2 on v1

--- a/solution.py
+++ b/solution.py
@@ -11,7 +11,7 @@
 SH_DEV = 64
 LANES = 128
 CHUNK = 512
-SLAB = 8
+SLAB = 16
 
 
 learn_rate = 0.1
@@ -25,12 +25,6 @@
     return jnp.dot(a, b, preferred_element_type=f32)
 
 
-def dot_split(a, b):
-    high = b.astype(bf16)
-    low = (b - high.astype(f32)).astype(bf16)
-    return dot(a, high) + dot(a, low)
-
-
 def columns(row):
     return jnp.transpose(jnp.broadcast_to(row.astype(f32), (LANES, row.shape[1])))
 
@@ -48,14 +42,20 @@
     groups,
     ent_ref,
     table_ref,
-    ids_ref,
-    list_ref,
+    src_ref,
+    dst_ref,
+    slots_ref,
+    neg_ref,
+    owner_ref,
+    row_ref,
     ent_state_ref,
     sh_state_ref,
     new_ent_ref,
     new_ent_state_ref,
     new_sh_ref,
     new_sh_state_ref,
+    ids_ref,
+    list_ref,
     vt_ref,
     pick_ref,
     slot_ref,
@@ -88,7 +88,7 @@
     devices = blks * reps
     me = blk * reps + rep
     rows, width = ent_ref.shape
-    buckets, edges = ids_ref.shape[0], ids_ref.shape[2]
+    buckets, edges = src_ref.shape[1:]
     group_edges = edges // groups
     chunks = rows // CHUNK
     highs = rows // LANES
@@ -110,6 +110,26 @@
         return 0
 
     lax.fori_loop(1, devices, greet, 0)
+
+    for bucket in range(buckets):
+        ids_ref[bucket, 0:1, :] = dst_ref[0, bucket : bucket + 1, :]
+        ids_ref[bucket, 1 : 1 + groups, :] = neg_ref[0, bucket]
+        ids_ref[bucket, 1 + groups : 2 + groups, :] = src_ref[0, bucket : bucket + 1, :]
+        ids_ref[bucket, 2 + groups : 3 + groups, :] = slots_ref[0, bucket : bucket + 1, :]
+        ids_ref[bucket, 3 + groups :, :] = jnp.zeros((8 - 3 - groups, edges), jnp.int32)
+    count = row_ref.shape[1]
+    owner_cols = jnp.broadcast_to(owner_ref[0].astype(f32), (count, LANES))
+    owners = jnp.transpose(owner_cols)[0:1, :]
+    same = jnp.broadcast_to(owner_ref[0].astype(f32), (count, count)) == owners
+    earlier = lax.broadcasted_iota(jnp.int32, (count, count), 0) < lax.broadcasted_iota(
+        jnp.int32, (count, count), 1
+    )
+    ranks = jnp.sum(jnp.where(same & earlier, 1.0, 0.0), axis=0, keepdims=True)
+    owners = owners.astype(jnp.int32)
+    list_ref[...] = jnp.full(list_ref.shape, -SH_DEV, jnp.int32)
+    list_ref[0:1, :count] = owners * SH_DEV + row_ref[...]
+    list_ref[1:2, :count] = owners * SLAB + ranks.astype(jnp.int32)
+    list_ref[2:3, :count] = row_ref[...]
 
     vt_ref[...] = jnp.transpose(ent_ref[...].astype(f32)).astype(bf16)
     id_cols = columns(list_ref[0:1, :])
@@ -157,19 +177,19 @@
         )
 
     def make_query(bucket):
-        slot = jnp.where(lane_hot(columns(ids_ref[bucket, 6:7, :]), 0, list_pad), 1.0, 0.0)
+        slot = jnp.where(lane_hot(columns(ids_ref[bucket, 2 + groups : 3 + groups, :]), 0, list_pad), 1.0, 0.0)
         slot_ref[bucket] = slot.astype(bf16)
-        dcol_ref[...] = columns(ids_ref[bucket, 5:6, :])
+        dcol_ref[...] = columns(ids_ref[bucket, 1 + groups : 2 + groups, :])
         qg_ref[...] = dot(slot_ref[bucket], shared_rows)
 
         def body(c, _):
             at = pl.multiple_of(c * CHUNK, CHUNK)
             pick = jnp.where(lane_hot(dcol_ref[...], at, CHUNK), 1.0, 0.0).astype(bf16)
-            pick_ref[bucket, :, pl.ds(at, CHUNK)] = pick
+            pick_ref[bucket * edges : (bucket + 1) * edges, pl.ds(at, CHUNK)] = pick
             qg_ref[...] += dot(pick, ent_ref[pl.ds(at, CHUNK), :])
             return 0
 
-        lax.fori_loop(0, chunks, body, 0)
+        lax.fori_loop(0, chunks, body, 0, unroll=True)
         q_out[bucket] = qg_ref[...].astype(bf16)
 
     def score(query_ref, id_ref, out_ref, first):
@@ -221,7 +241,7 @@
                 gt_ref[:, pl.ds(at, CHUNK)] += grown
             return 0
 
-        lax.fori_loop(0, chunks, body, 0)
+        lax.fori_loop(0, chunks, body, 0, unroll=True)
         out_ref[...] = jnp.transpose(qg_ref[...]).astype(bf16)
 
     make_query(1)
@@ -240,21 +260,14 @@
         score(q_in.at[bucket], ids_in.at[bucket], qg_out.at[bucket], False)
         grad_copy(bucket).start()
 
-    slot_total = jnp.zeros((width, list_pad), f32)
-    for bucket in range(buckets):
-        if bucket:
-            grad_copy(bucket).wait_recv()
-            back = qg_in[bucket]
-        else:
-            back = qg_out[0]
-        slot_total = slot_total + dot(back, slot_ref[bucket])
-
-        def body(c, _, back=back, bucket=bucket):
-            at = pl.ds(pl.multiple_of(c * CHUNK, CHUNK), CHUNK)
-            gt_ref[:, at] += dot(back, pick_ref[bucket, :, at])
-            return 0
-
-        lax.fori_loop(0, chunks, body, 0)
+    for bucket in range(1, buckets):
+        grad_copy(bucket).wait_recv()
+    backs = [qg_out[0]] + [qg_in[bucket] for bucket in range(1, buckets)]
+    backs = jnp.concatenate(backs, axis=1)
+
+    def share_grad(peer):
+        at = pl.ds(pl.multiple_of(peer * share, share), share)
+        return gt_ref[:, at] + dot(backs, pick_ref[:, at])
 
     def share_copy(peer):
         return pltpu.make_async_remote_copy(
@@ -268,17 +281,23 @@
 
     for off in range(1, reps):
         peer = lax.rem(rep + off, reps)
-        at = pl.ds(pl.multiple_of(peer * share, share), share)
-        rs_out[peer] = gt_ref[:, at].astype(bf16)
+        rs_out[peer] = share_grad(peer).astype(bf16)
         share_copy(peer).start()
 
+    slot_total = jnp.zeros((width, list_pad), f32)
+    for bucket in range(buckets):
+        back = backs[:, bucket * edges : (bucket + 1) * edges]
+        slot_total = slot_total + dot(back, slot_ref[bucket])
+    slot_total = jnp.transpose(slot_total).astype(bf16)
+    places = lax.broadcasted_iota(jnp.int32, (devices * SLAB, list_pad), 0)
     keys = list_ref[1:2, :]
-    hot = lax.broadcasted_iota(jnp.int32, (devices * SLAB, list_pad), 0) == keys
-    sh_out[:, :width] = dot_split(
-        jnp.where(hot, 1.0, 0.0).astype(bf16), jnp.transpose(slot_total)
-    )
-    marks = jnp.where(hot, list_ref[2:3, :].astype(f32), 0.0).astype(bf16)
-    sh_out[:, width:] = dot(marks, jnp.ones((list_pad, LANES), bf16))
+    marks = jnp.where(places == keys + 2 * CAP, list_ref[2:3, :].astype(f32), 0.0).astype(bf16)
+    block = dot(marks, jnp.ones((list_pad, LANES), bf16))
+    for half in range(width // LANES):
+        hot = jnp.where(places == keys + half * CAP, 1.0, 0.0).astype(bf16)
+        block = block + dot(hot, slot_total[:, half * LANES : (half + 1) * LANES])
+    sh_out[...] = block.astype(bf16)
+    own_grad = share_grad(rep)
 
     def slab(ref, peer):
         return ref.at[pl.ds(pl.multiple_of(peer * SLAB, SLAB), SLAB), :]
@@ -314,16 +333,25 @@
         return 0
 
     lax.fori_loop(1, devices, slab_wait, 0)
-    labels = jnp.transpose(sh_in[:, width:])[:SH_DEV, :]
+    inbound = sh_in[...]
+    labels = jnp.transpose(inbound.astype(f32))[:SH_DEV, :]
+    offset = lax.rem(lax.broadcasted_iota(jnp.int32, labels.shape, 1), SLAB)
     hot = labels == lax.broadcasted_iota(jnp.int32, labels.shape, 0).astype(f32)
-    shared_grad = dot_split(jnp.where(hot, 1.0, 0.0).astype(bf16), sh_in[:, :width])
-    new_state = sh_state_ref[...] + jnp.mean(shared_grad * shared_grad, axis=1, keepdims=True)
-    new_sh_state_ref[...] = new_state
+    hot = jnp.where(hot & (offset >= 2 * CAP) & (offset < 3 * CAP), 1.0, 0.0)
+    halves = []
+    for half in range(width // LANES):
+        moved = pltpu.roll(hot, hot.shape[1] - (2 - half) * CAP, 1)
+        halves.append(dot(moved.astype(bf16), inbound))
+    shared_grad = jnp.concatenate(halves, axis=1)
+    state_cols = jnp.transpose(jnp.broadcast_to(sh_state_ref[...], (LANES, SH_DEV)))
+    means = jnp.mean(shared_grad * shared_grad, axis=1, keepdims=True)
+    new_state = state_cols + means
+    new_sh_state_ref[...] = jnp.transpose(new_state)[0:1, :]
     own_shared = table_ref[pl.ds(pl.multiple_of(me * SH_DEV, SH_DEV), SH_DEV), :].astype(f32)
-    new_sh_ref[...] = own_shared - learn_rate * shared_grad / jnp.sqrt(new_state)
+    new_sh_ref[...] = own_shared - learn_rate * shared_grad / jnp.sqrt(tiled(new_state, width))
 
     own = pl.ds(pl.multiple_of(rep * share, share), share)
-    grad = gt_ref[:, own]
+    grad = own_grad
     for off in range(1, reps):
         peer = lax.rem(rep + reps - off, reps)
         pltpu.make_async_remote_copy(
@@ -363,24 +391,7 @@
     share = rows // reps
     buckets, edges = edge_src.shape[1:]
     groups = neg_rows.shape[2]
-    owners = list_owner[0, :, 0]
-    count = owners.shape[0]
-    list_pad = -(-count // LANES) * LANES
-    order = jnp.arange(count, dtype=jnp.int32)
-    earlier = (owners[:, None] == owners[None, :]) & (order[:, None] < order[None, :])
-    ranks = jnp.sum(earlier.astype(jnp.int32), axis=0)
-    lists = jnp.stack([owners * SH_DEV + list_row[0], owners * SLAB + ranks, list_row[0]])
-    lists = jnp.pad(lists, ((0, 5), (0, list_pad - count)), constant_values=-1)
-    ids = jnp.concatenate(
-        [
-            edge_dst[0][:, None],
-            neg_rows[0],
-            edge_src[0][:, None],
-            edge_slot[0][:, None],
-            jnp.zeros((buckets, 1, edges), jnp.int32),
-        ],
-        axis=1,
-    )
+    list_pad = -(-list_row.shape[1] // LANES) * LANES
     sems = pltpu.SemaphoreType.DMA
     vmem = pl.BlockSpec(memory_space=pltpu.VMEM)
     new_entities, new_entity_state, new_shared, new_shared_state = pl.pallas_call(
@@ -389,13 +400,15 @@
             jax.ShapeDtypeStruct((share, width), f32),
             jax.ShapeDtypeStruct((1, share), f32),
             jax.ShapeDtypeStruct((SH_DEV, width), f32),
-            jax.ShapeDtypeStruct((SH_DEV, 1), f32),
+            jax.ShapeDtypeStruct((1, SH_DEV), f32),
         ),
-        in_specs=[vmem] * 6,
+        in_specs=[vmem] * 10,
         out_specs=[vmem] * 4,
         scratch_shapes=[
+            pltpu.VMEM((buckets, 8, edges), jnp.int32),
+            pltpu.VMEM((8, list_pad), jnp.int32),
             pltpu.VMEM((width, rows), bf16),
-            pltpu.VMEM((buckets, edges, rows), bf16),
+            pltpu.VMEM((buckets * edges, rows), bf16),
             pltpu.VMEM((buckets, edges, list_pad), bf16),
             pltpu.VMEM((buckets, edges, width), bf16),
             pltpu.VMEM((buckets, edges, width), bf16),
@@ -408,8 +421,8 @@
             pltpu.VMEM((width, rows), f32),
             pltpu.VMEM((reps, width, share), bf16),
             pltpu.VMEM((reps, width, share), bf16),
-            pltpu.VMEM((devices * SLAB, width + LANES), f32),
-            pltpu.VMEM((devices * SLAB, width + LANES), f32),
+            pltpu.VMEM((devices * SLAB, LANES), bf16),
+            pltpu.VMEM((devices * SLAB, LANES), bf16),
             sems((buckets,)),
             sems((buckets,)),
             sems((buckets,)),
@@ -427,10 +440,14 @@
     )(
         entities,
         shared_table,
-        ids,
-        lists,
+        edge_src,
+        edge_dst,
+        edge_slot,
+        neg_rows,
+        list_owner,
+        list_row,
         entity_state.reshape(1, share),
-        shared_state.reshape(SH_DEV, 1),
+        shared_state.reshape(1, SH_DEV),
     )
     return (
         new_entities,

time: 80.1 us -> 71.4 us (0.89)
  Pallas kernels: 71.1 us -> 65.5 us
  other arithmetic: 1.49 us -> 0 us
  local copies, waits for them, and re-layouts: 6.47 us -> 4.99 us
    pallas_call x1, Pallas kernels: 71.1 us -> 65.5 us  [shards(): pl.pallas_call(functools.partial(kernel, groups), out_shape=(jax.ShapeDty...]
    pallas_call x1 -> x0, other arithmetic: 1.39 us -> none  [shards(): pl.pallas_call(functools.partial(kernel, groups), out_shape=(jax.ShapeDty...]
    unnamed x21 -> x13, local copies, waits for them, and re-layouts: 4.45 us -> 4.99 us
where the time goes in v2:
time: 71.4 us; the launch traced here: 71.2 us
  Pallas kernels  65.5 us (92%)
  local copies, waits for them, and re-layouts  4.99 us (7%)
    pallas_call x1, Pallas kernels, shards(): pl.pallas_call(functools.partial(kernel, groups), out_shape=(jax.ShapeDty...  65.5 us
    unnamed x13, local copies, waits for them, and re-layouts  4.99 us

profile of v2, /device:TPU:0, one launch (start us, length us, event | category | flops | bytes accessed | tf_op | source)
XLA Modules:
  0.0 71.2 jit_solution(22376468956225930)
XLA Ops:
  0.6 0.0 copy-start.2
  0.6 0.6 copy-done.2
  1.3 0.7 copy.14.owner_ref
  2.0 65.5 %shard_map.129 = (f32[512,256]{1,0:T(8,128)}, f32[1,512]{1,0:T(1,128)}, f32[64,256]{1,0:T(8,128)}, f32[1,64]{1,0:T(1,128)}) custom-call(bf16[2048,256]{1,0:T(8,128)(2,1)} %ent_ref.1, bf16[2048,256]{1,0:T(8,128)(2,1)} %table_ref.1, s32[1,4,512]{2,1,0:T(4,128)} %src_ref.1, s32[1,4,512]{2,1,0:T(4,128)} %dst_ref.1, s32[1,4,512]{2,1,0:T(4,128)} %slots_ref.1, ...), custom_call_target="tpu_custom_call" | custom-call | tf_op jit(solution)/shard_map/pallas_call | solution.py:397
  67.5 0.0 copy-start.1
  67.5 0.0 copy-start
  67.5 1.9 %copy.19 = f32[512,256]{1,0:T(8,128)} copy(f32[512,256]{1,0:T(8,128)} %get-tuple-element.16) | data formatting | bytes 1048576
  69.5 0.0 copy-done.1
  69.5 0.6 copy.20
  70.0 0.0 copy-done
  70.0 0.0 copy-start.3
  70.0 0.6 copy.21
  70.7 0.0 copy-done.3
  70.7 0.5 copy.22
Async XLA Ops:
  0.6 0.7 copy-start.2
  67.5 1.9 %copy-start.1 = (f32[1,512]{1,0:T(1,128)S(1)}, f32[1,512]{1,0:T(1,128)}, u32[]{:S(2)}) copy-start(f32[1,512]{1,0:T(1,128)} %get-tuple-element.9) | copy-start | bytes 6148
  67.5 2.5 %copy-start = (f32[64,256]{1,0:T(8,128)S(1)}, f32[64,256]{1,0:T(8,128)}, u32[]{:S(2)}) copy-start(f32[64,256]{1,0:T(8,128)} %get-tuple-element.18) | copy-start | bytes 196612
  70.0 0.6 copy-start.3

commit v3 on v2

--- a/solution.py
+++ b/solution.py
@@ -10,6 +10,7 @@
 CAP = 4
 SH_DEV = 64
 LANES = 128
+HALVES = 2
 CHUNK = 512
 SLAB = 16
 
@@ -93,6 +94,7 @@
     chunks = rows // CHUNK
     highs = rows // LANES
     share = rows // reps
+    part = width // HALVES
     list_pad = list_ref.shape[1]
 
     def place(peer):
@@ -118,14 +120,13 @@
         ids_ref[bucket, 2 + groups : 3 + groups, :] = slots_ref[0, bucket : bucket + 1, :]
         ids_ref[bucket, 3 + groups :, :] = jnp.zeros((8 - 3 - groups, edges), jnp.int32)
     count = row_ref.shape[1]
-    owner_cols = jnp.broadcast_to(owner_ref[0].astype(f32), (count, LANES))
-    owners = jnp.transpose(owner_cols)[0:1, :]
-    same = jnp.broadcast_to(owner_ref[0].astype(f32), (count, count)) == owners
+    owners = owner_ref[...]
+    owner_cols = jnp.concatenate([columns(owners)] * (list_ref.shape[1] // LANES), axis=1)
+    same = owner_cols[:, :count] == owners.astype(f32)
     earlier = lax.broadcasted_iota(jnp.int32, (count, count), 0) < lax.broadcasted_iota(
         jnp.int32, (count, count), 1
     )
     ranks = jnp.sum(jnp.where(same & earlier, 1.0, 0.0), axis=0, keepdims=True)
-    owners = owners.astype(jnp.int32)
     list_ref[...] = jnp.full(list_ref.shape, -SH_DEV, jnp.int32)
     list_ref[0:1, :count] = owners * SH_DEV + row_ref[...]
     list_ref[1:2, :count] = owners * SLAB + ranks.astype(jnp.int32)
@@ -166,12 +167,13 @@
             device_id_type=MESH,
         )
 
-    def grad_copy(bucket):
+    def grad_copy(bucket, half):
+        place = half * buckets + bucket
         return pltpu.make_async_remote_copy(
-            src_ref=qg_out.at[bucket],
-            dst_ref=qg_in.at[bucket],
-            send_sem=g_send.at[bucket],
-            recv_sem=g_recv.at[bucket],
+            src_ref=qg_out.at[place],
+            dst_ref=qg_in.at[place],
+            send_sem=g_send.at[place],
+            recv_sem=g_recv.at[place],
             device_id=to_front(bucket),
             device_id_type=MESH,
         )
@@ -192,7 +194,7 @@
         lax.fori_loop(0, chunks, body, 0, unroll=True)
         q_out[bucket] = qg_ref[...].astype(bf16)
 
-    def score(query_ref, id_ref, out_ref, first):
+    def score(query_ref, id_ref, bucket):
         query = query_ref[...]
         query_t = jnp.transpose(query.astype(f32)).astype(bf16)
         dcol_ref[...] = columns(id_ref[0:1, :])
@@ -235,14 +237,16 @@
             weight = jnp.where(target, sampled + sigmoid - 1.0, sampled).astype(bf16)
             qg_ref[...] += dot(weight, ent_ref[pl.ds(at, CHUNK), :])
             grown = dot(query_t, weight)
-            if first:
+            if bucket == 0:
                 gt_ref[:, pl.ds(at, CHUNK)] = grown
             else:
                 gt_ref[:, pl.ds(at, CHUNK)] += grown
             return 0
 
         lax.fori_loop(0, chunks, body, 0, unroll=True)
-        out_ref[...] = jnp.transpose(qg_ref[...]).astype(bf16)
+        grads = jnp.transpose(qg_ref[...]).astype(bf16)
+        for half in range(HALVES):
+            qg_out[half * buckets + bucket] = grads[half * part : (half + 1) * part, :]
 
     make_query(1)
     pl.semaphore_wait(barrier, devices - 1)
@@ -253,36 +257,46 @@
             make_query(bucket)
         query_copy(bucket).start()
     make_query(0)
-    score(q_out.at[0], ids_ref.at[0], qg_out.at[0], True)
+    score(q_out.at[0], ids_ref.at[0], 0)
     for bucket in range(1, buckets):
         id_copy(bucket).wait_recv()
         query_copy(bucket).wait_recv()
-        score(q_in.at[bucket], ids_in.at[bucket], qg_out.at[bucket], False)
-        grad_copy(bucket).start()
-
-    for bucket in range(1, buckets):
-        grad_copy(bucket).wait_recv()
-    backs = [qg_out[0]] + [qg_in[bucket] for bucket in range(1, buckets)]
-    backs = jnp.concatenate(backs, axis=1)
-
-    def share_grad(peer):
-        at = pl.ds(pl.multiple_of(peer * share, share), share)
-        return gt_ref[:, at] + dot(backs, pick_ref[:, at])
-
-    def share_copy(peer):
+        score(q_in.at[bucket], ids_in.at[bucket], bucket)
+        grad_copy(bucket, 0).start()
+    for half in range(1, HALVES):
+        for bucket in range(1, buckets):
+            grad_copy(bucket, half).start()
+
+    def share_copy(peer, half, slot):
         return pltpu.make_async_remote_copy(
-            src_ref=rs_out.at[peer],
-            dst_ref=rs_in.at[rep],
-            send_sem=r_send.at[peer],
-            recv_sem=r_recv.at[rep],
+            src_ref=rs_out.at[half * reps + peer],
+            dst_ref=rs_in.at[half * reps + slot],
+            send_sem=r_send.at[half * reps + peer],
+            recv_sem=r_recv.at[half * reps + slot],
             device_id=(blk, peer),
             device_id_type=MESH,
         )
 
-    for off in range(1, reps):
-        peer = lax.rem(rep + off, reps)
-        rs_out[peer] = share_grad(peer).astype(bf16)
-        share_copy(peer).start()
+    backs, own_grad = [], []
+    for half in range(HALVES):
+        for bucket in range(1, buckets):
+            grad_copy(bucket, half).wait_recv()
+        back = [qg_out[half * buckets]]
+        back = back + [qg_in[half * buckets + bucket] for bucket in range(1, buckets)]
+        back = jnp.concatenate(back, axis=1)
+        backs.append(back)
+
+        def share_grad(peer, half=half, back=back):
+            at = pl.ds(pl.multiple_of(peer * share, share), share)
+            return gt_ref[half * part : (half + 1) * part, at] + dot(back, pick_ref[:, at])
+
+        for off in range(1, reps):
+            peer = lax.rem(rep + off, reps)
+            rs_out[half * reps + peer] = share_grad(peer).astype(bf16)
+            share_copy(peer, half, rep).start()
+        own_grad.append(share_grad(rep))
+    own_grad = jnp.concatenate(own_grad, axis=0)
+    backs = jnp.concatenate(backs, axis=0)
 
     slot_total = jnp.zeros((width, list_pad), f32)
     for bucket in range(buckets):
@@ -297,7 +311,6 @@
         hot = jnp.where(places == keys + half * CAP, 1.0, 0.0).astype(bf16)
         block = block + dot(hot, slot_total[:, half * LANES : (half + 1) * LANES])
     sh_out[...] = block.astype(bf16)
-    own_grad = share_grad(rep)
 
     def slab(ref, peer):
         return ref.at[pl.ds(pl.multiple_of(peer * SLAB, SLAB), SLAB), :]
@@ -354,15 +367,11 @@
     grad = own_grad
     for off in range(1, reps):
         peer = lax.rem(rep + reps - off, reps)
-        pltpu.make_async_remote_copy(
-            src_ref=rs_out.at[peer],
-            dst_ref=rs_in.at[peer],
-            send_sem=r_send.at[peer],
-            recv_sem=r_recv.at[peer],
-            device_id=(blk, peer),
-            device_id_type=MESH,
-        ).wait()
-        grad = grad + rs_in[peer].astype(f32)
+        arrived = []
+        for half in range(HALVES):
+            share_copy(peer, half, peer).wait()
+            arrived.append(rs_in[half * reps + peer].astype(f32))
+        grad = grad + jnp.concatenate(arrived, axis=0)
     new_state = ent_state_ref[...] + jnp.mean(grad * grad, axis=0, keepdims=True)
     new_ent_state_ref[...] = new_state
     update = jnp.transpose(learn_rate * grad / jnp.sqrt(new_state))
@@ -370,7 +379,8 @@
     for bucket in range(1, buckets):
         id_copy(bucket).wait_send()
         query_copy(bucket).wait_send()
-        grad_copy(bucket).wait_send()
+        for half in range(HALVES):
+            grad_copy(bucket, half).wait_send()
 
 
 def shards(
@@ -413,24 +423,24 @@
             pltpu.VMEM((buckets, edges, width), bf16),
             pltpu.VMEM((buckets, edges, width), bf16),
             pltpu.VMEM((buckets, 8, edges), jnp.int32),
-            pltpu.VMEM((buckets, width, edges), bf16),
-            pltpu.VMEM((buckets, width, edges), bf16),
+            pltpu.VMEM((HALVES * buckets, width // HALVES, edges), bf16),
+            pltpu.VMEM((HALVES * buckets, width // HALVES, edges), bf16),
             pltpu.VMEM((edges, LANES), f32),
             pltpu.VMEM((groups * (rows // LANES), LANES), f32),
             pltpu.VMEM((edges, width), f32),
             pltpu.VMEM((width, rows), f32),
-            pltpu.VMEM((reps, width, share), bf16),
-            pltpu.VMEM((reps, width, share), bf16),
+            pltpu.VMEM((HALVES * reps, width // HALVES, share), bf16),
+            pltpu.VMEM((HALVES * reps, width // HALVES, share), bf16),
             pltpu.VMEM((devices * SLAB, LANES), bf16),
             pltpu.VMEM((devices * SLAB, LANES), bf16),
             sems((buckets,)),
             sems((buckets,)),
             sems((buckets,)),
             sems((buckets,)),
-            sems((buckets,)),
-            sems((buckets,)),
-            sems((reps,)),
-            sems((reps,)),
+            sems((HALVES * buckets,)),
+            sems((HALVES * buckets,)),
+            sems((HALVES * reps,)),
+            sems((HALVES * reps,)),
             sems((devices,)),
             sems((devices,)),
         ],
@@ -444,7 +454,7 @@
         edge_dst,
         edge_slot,
         neg_rows,
-        list_owner,
+        list_owner.reshape(list_row.shape),
         list_row,
         entity_state.reshape(1, share),
         shared_state.reshape(1, SH_DEV),

time: 71.4 us -> 67.3 us (0.943)
  Pallas kernels: 65.5 us -> 62.8 us
  local copies, waits for them, and re-layouts: 4.99 us -> 3.66 us
    pallas_call x1, Pallas kernels: 65.5 us -> 62.8 us  [shards(): pl.pallas_call(functools.partial(kernel, groups), out_shape=(jax.ShapeDty...]
    unnamed x13 -> x10, local copies, waits for them, and re-layouts: 4.99 us -> 3.66 us
where the time goes in v3:
time: 67.3 us; the launch traced here: 67.1 us
  Pallas kernels  62.8 us (93%)
  local copies, waits for them, and re-layouts  3.66 us (5%)
    pallas_call x1, Pallas kernels, shards(): pl.pallas_call(functools.partial(kernel, groups), out_shape=(jax.ShapeDty...  62.8 us
    unnamed x10, local copies, waits for them, and re-layouts  3.66 us

profile of v3, /device:TPU:0, one launch (start us, length us, event | category | flops | bytes accessed | tf_op | source)
XLA Modules:
  0.0 67.1 jit_solution(6637398310136521006)
XLA Ops:
  0.6 62.8 %shard_map.129 = (f32[512,256]{1,0:T(8,128)}, f32[1,512]{1,0:T(1,128)}, f32[64,256]{1,0:T(8,128)}, f32[1,64]{1,0:T(1,128)}) custom-call(bf16[2048,256]{1,0:T(8,128)(2,1)} %ent_ref.1, bf16[2048,256]{1,0:T(8,128)(2,1)} %table_ref.1, s32[1,4,512]{2,1,0:T(4,128)} %src_ref.1, s32[1,4,512]{2,1,0:T(4,128)} %dst_ref.1, s32[1,4,512]{2,1,0:T(4,128)} %slots_ref.1, ...), custom_call_target="tpu_custom_call" | custom-call | tf_op jit(solution)/shard_map/pallas_call | solution.py:407
  63.5 0.0 copy-start.1
  63.5 0.0 copy-start
  63.5 1.9 %copy.18 = f32[512,256]{1,0:T(8,128)} copy(f32[512,256]{1,0:T(8,128)} %get-tuple-element.16) | data formatting | bytes 1048576
  65.4 0.0 copy-done.1
  65.4 0.6 copy.19
  66.0 0.0 copy-done
  66.0 0.0 copy-start.2
  66.0 0.6 copy.20
  66.6 0.0 copy-done.2
  66.6 0.5 copy.21
Async XLA Ops:
  63.5 1.9 %copy-start.1 = (f32[1,512]{1,0:T(1,128)S(1)}, f32[1,512]{1,0:T(1,128)}, u32[]{:S(2)}) copy-start(f32[1,512]{1,0:T(1,128)} %get-tuple-element.9) | copy-start | bytes 6148
  63.5 2.5 %copy-start = (f32[64,256]{1,0:T(8,128)S(1)}, f32[64,256]{1,0:T(8,128)}, u32[]{:S(2)}) copy-start(f32[64,256]{1,0:T(8,128)} %get-tuple-element.18) | copy-start | bytes 196612
  66.0 0.7 copy-start.2

commit v4 on v3

--- a/solution.py
+++ b/solution.py
@@ -70,7 +70,9 @@
     qg_ref,
     gt_ref,
     rs_out,
-    rs_in,
+    rs_up,
+    rs_down,
+    own_ref,
     sh_out,
     sh_in,
     q_send,
@@ -80,7 +82,8 @@
     g_send,
     g_recv,
     r_send,
-    r_recv,
+    up_recv,
+    down_recv,
     s_send,
     s_recv,
 ):
@@ -267,17 +270,38 @@
         for bucket in range(1, buckets):
             grad_copy(bucket, half).start()
 
-    def share_copy(peer, half, slot):
+    def share_copy(half, peer, up):
+        at = half * reps + peer
         return pltpu.make_async_remote_copy(
-            src_ref=rs_out.at[half * reps + peer],
-            dst_ref=rs_in.at[half * reps + slot],
-            send_sem=r_send.at[half * reps + peer],
-            recv_sem=r_recv.at[half * reps + slot],
-            device_id=(blk, peer),
+            src_ref=rs_out.at[at],
+            dst_ref=(rs_up if up else rs_down).at[at],
+            send_sem=r_send.at[at],
+            recv_sem=(up_recv if up else down_recv).at[at],
+            device_id=(blk, lax.rem(rep + (1 if up else reps - 1), reps)),
             device_id_type=MESH,
         )
 
-    backs, own_grad = [], []
+    def pass_share(half, peer, up, taken, share_grad):
+        at = half * reps + peer
+        first = rep == (0 if up else reps - 1)
+
+        @pl.when(taken & (rep < peer if up else rep > peer))
+        def _():
+            total = share_grad(peer)
+
+            @pl.when(first)
+            def _():
+                rs_out[at] = total.astype(bf16)
+
+            @pl.when(jnp.logical_not(first))
+            def _():
+                share_copy(half, peer, up).wait_recv()
+                rs_out[at] = (total + (rs_up if up else rs_down)[at].astype(f32)).astype(bf16)
+
+            share_copy(half, peer, up).start()
+
+    backs = []
+    low_end = rep < reps // 2
     for half in range(HALVES):
         for bucket in range(1, buckets):
             grad_copy(bucket, half).wait_recv()
@@ -290,12 +314,11 @@
             at = pl.ds(pl.multiple_of(peer * share, share), share)
             return gt_ref[half * part : (half + 1) * part, at] + dot(back, pick_ref[:, at])
 
-        for off in range(1, reps):
-            peer = lax.rem(rep + off, reps)
-            rs_out[half * reps + peer] = share_grad(peer).astype(bf16)
-            share_copy(peer, half, rep).start()
-        own_grad.append(share_grad(rep))
-    own_grad = jnp.concatenate(own_grad, axis=0)
+        for hop in range(reps - 1):
+            pass_share(half, reps - 1 - hop, True, low_end, share_grad)
+            pass_share(half, hop, False, rep >= 0, share_grad)
+            pass_share(half, reps - 1 - hop, True, jnp.logical_not(low_end), share_grad)
+        own_ref[half * part : (half + 1) * part, :] = share_grad(rep)
     backs = jnp.concatenate(backs, axis=0)
 
     slot_total = jnp.zeros((width, list_pad), f32)
@@ -364,14 +387,16 @@
     new_sh_ref[...] = own_shared - learn_rate * shared_grad / jnp.sqrt(tiled(new_state, width))
 
     own = pl.ds(pl.multiple_of(rep * share, share), share)
-    grad = own_grad
-    for off in range(1, reps):
-        peer = lax.rem(rep + reps - off, reps)
-        arrived = []
-        for half in range(HALVES):
-            share_copy(peer, half, peer).wait()
-            arrived.append(rs_in[half * reps + peer].astype(f32))
-        grad = grad + jnp.concatenate(arrived, axis=0)
+    for up in (True, False):
+
+        @pl.when((rep > 0) if up else (rep < reps - 1))
+        def _(up=up):
+            for half in range(HALVES):
+                share_copy(half, rep, up).wait_recv()
+                arrived = (rs_up if up else rs_down)[half * reps + rep]
+                own_ref[half * part : (half + 1) * part, :] += arrived.astype(f32)
+
+    grad = own_ref[...]
     new_state = ent_state_ref[...] + jnp.mean(grad * grad, axis=0, keepdims=True)
     new_ent_state_ref[...] = new_state
     update = jnp.transpose(learn_rate * grad / jnp.sqrt(new_state))
@@ -381,6 +406,12 @@
         query_copy(bucket).wait_send()
         for half in range(HALVES):
             grad_copy(bucket, half).wait_send()
+    for peer in range(reps):
+
+        @pl.when(rep != peer)
+        def _(peer=peer):
+            for half in range(HALVES):
+                share_copy(half, peer, True).wait_send()
 
 
 def shards(
@@ -431,6 +462,8 @@
             pltpu.VMEM((width, rows), f32),
             pltpu.VMEM((HALVES * reps, width // HALVES, share), bf16),
             pltpu.VMEM((HALVES * reps, width // HALVES, share), bf16),
+            pltpu.VMEM((HALVES * reps, width // HALVES, share), bf16),
+            pltpu.VMEM((width, share), f32),
             pltpu.VMEM((devices * SLAB, LANES), bf16),
             pltpu.VMEM((devices * SLAB, LANES), bf16),
             sems((buckets,)),
@@ -439,6 +472,7 @@
             sems((buckets,)),
             sems((HALVES * buckets,)),
             sems((HALVES * buckets,)),
+            sems((HALVES * reps,)),
             sems((HALVES * reps,)),
             sems((HALVES * reps,)),
             sems((devices,)),

time: 67.3 us -> 64.2 us (0.954)
  Pallas kernels: 62.8 us -> 59.7 us
    pallas_call x1, Pallas kernels: 62.8 us -> 59.7 us  [shards(): pl.pallas_call(functools.partial(kernel, groups), out_shape=(jax.ShapeDty...]
where the time goes in v4:
time: 64.2 us; the launch traced here: 64 us
  Pallas kernels  59.7 us (93%)
  local copies, waits for them, and re-layouts  3.66 us (6%)
  between operations  0.66 us (1%)
    pallas_call x1, Pallas kernels, shards(): pl.pallas_call(functools.partial(kernel, groups), out_shape=(jax.ShapeDty...  59.7 us
    unnamed x10, local copies, waits for them, and re-layouts  3.66 us

profile of v4, /device:TPU:0, one launch (start us, length us, event | category | flops | bytes accessed | tf_op | source)
XLA Modules:
  0.0 64.0 jit_solution(11307012099857967165)
XLA Ops:
  0.6 59.7 %shard_map.129 = (f32[512,256]{1,0:T(8,128)}, f32[1,512]{1,0:T(1,128)}, f32[64,256]{1,0:T(8,128)}, f32[1,64]{1,0:T(1,128)}) custom-call(bf16[2048,256]{1,0:T(8,128)(2,1)} %ent_ref.1, bf16[2048,256]{1,0:T(8,128)(2,1)} %table_ref.1, s32[1,4,512]{2,1,0:T(4,128)} %src_ref.1, s32[1,4,512]{2,1,0:T(4,128)} %dst_ref.1, s32[1,4,512]{2,1,0:T(4,128)} %slots_ref.1, ...), custom_call_target="tpu_custom_call" | custom-call | tf_op jit(solution)/shard_map/pallas_call | solution.py:438
  60.3 0.0 copy-start.1
  60.3 0.0 copy-start
  60.3 1.9 %copy.18 = f32[512,256]{1,0:T(8,128)} copy(f32[512,256]{1,0:T(8,128)} %get-tuple-element.16) | data formatting | bytes 1048576
  62.2 0.0 copy-done.1
  62.2 0.6 copy.19
  62.8 0.0 copy-done
  62.8 0.0 copy-start.2
  62.8 0.6 copy.20
  63.5 0.0 copy-done.2
  63.5 0.5 copy.21
Async XLA Ops:
  60.3 1.9 %copy-start.1 = (f32[1,512]{1,0:T(1,128)S(1)}, f32[1,512]{1,0:T(1,128)}, u32[]{:S(2)}) copy-start(f32[1,512]{1,0:T(1,128)} %get-tuple-element.9) | copy-start | bytes 6148
  60.3 2.5 %copy-start = (f32[64,256]{1,0:T(8,128)S(1)}, f32[64,256]{1,0:T(8,128)}, u32[]{:S(2)}) copy-start(f32[64,256]{1,0:T(8,128)} %get-tuple-element.18) | copy-start | bytes 196612
  62.8 0.7 %copy-start.2 = (f32[1,64]{1,0:T(1,128)S(1)}, f32[1,64]{1,0:T(1,128)}, u32[]{:S(2)}) copy-start(f32[1,64]{1,0:T(1,128)} %get-tuple-element.11) | copy-start | bytes 772
